TPU v7x, 32 devices: a whole 2x2x4 slice. The times are simulated.
32 devices in a mesh: events: 4 (over z), nodes: 8 (over y, x, core).
Axes of the slice: x: 2, y: 2, z: 4, core: 2. Of those that a mesh axis runs over, the one named last changes fastest.
Arguments:
- nodes_in: bfloat16 [4, 16384, 128], P('events', 'nodes'), may hold values from -6 to 6
- edge_latents: bfloat16 [4, 8, 8, 2, 128, 128], P('events', 'nodes'), may hold values from -6 to 6
- src_block: int32 [4, 8, 8, 2], P('events', 'nodes'), may hold values from 0 to 15
- src_offset: int32 [4, 8, 8, 2, 128], P('events', 'nodes'), may hold values from 0 to 127
- dst_block: int32 [4, 8, 8, 2], P('events', 'nodes'), may hold values from 0 to 15
- dst_offset: int32 [4, 8, 8, 2, 128], P('events', 'nodes'), may hold values from 0 to 127
- tile_counts: int32 [4, 8, 8], P('events'), may hold values from 1 to 2, as said below
- w_edge1: bfloat16 [384, 128], replicated, may hold values from -0.3125 to 0.3125
- b_edge1: float32 [128], replicated, may hold values from -3 to 3
- w_edge2: bfloat16 [128, 128], replicated, may hold values from -0.5 to 0.5
- b_edge2: float32 [128], replicated, may hold values from -3 to 3
- w_node1: bfloat16 [256, 128], replicated, may hold values from -0.375 to 0.375
- b_node1: float32 [128], replicated, may hold values from -3 to 3
- w_node2: bfloat16 [128, 128], replicated, may hold values from -0.5 to 0.5
- b_node2: float32 [128], replicated, may hold values from -3 to 3
- cotangent: bfloat16 [4, 16384, 128], P('events', 'nodes'), may hold values from -6 to 6
Outputs:
- new_nodes: bfloat16 [4, 16384, 128], P('events', 'nodes')
- node_grads: bfloat16 [4, 16384, 128], P('events', 'nodes')
- grad_w_edge1: float32 [384, 128], replicated
- grad_b_edge1: float32 [128], replicated
- grad_w_edge2: float32 [128, 128], replicated
- grad_b_edge2: float32 [128], replicated
- grad_w_node1: float32 [256, 128], replicated
- grad_b_node1: float32 [128], replicated
- grad_w_node2: float32 [128, 128], replicated
- grad_b_node2: float32 [128], replicated
Inputs may be any that keep to these rules, and one draw needn't show every extreme that they name: tile_counts[g, s, d] is the number of live slots from source device s to destination device d; in every event group some destination device receives exactly 2 tiles from every source device.
All inputs are finite; a program needn't handle non-finite values.
Results may differ from a plain program's by a relative error of at most 0.0067.
Values may be sent and summed in bfloat16 or wider, within the bound.
A program may use at most 64 MiB of HBM per device.

v0:
```python
import jax
import jax.numpy as jnp
from jax import lax
from jax.sharding import PartitionSpec as P


def silu_slope(value):
    sig = jax.nn.sigmoid(value)
    return sig * (1.0 + value * (1.0 - sig))


def tile_onehot(offsets, tile):
    return (offsets[..., None] == jnp.arange(tile, dtype=jnp.int32)[None, None, :]).astype(
        jnp.bfloat16
    )


def gather_tiles(table, blocks, onehot):
    tile = onehot.shape[-1]
    picked = table.reshape(-1, tile, table.shape[-1])[blocks]
    return jnp.einsum("ten,tnd->ted", onehot, picked, preferred_element_type=jnp.float32).astype(
        table.dtype
    )


def scatter_tiles(values, blocks, onehot, block_count):
    if values.dtype == jnp.bfloat16:
        per_tile = jnp.einsum("ten,ted->tnd", onehot, values, preferred_element_type=jnp.float32)
    else:
        per_tile = jnp.einsum(
            "ten,ted->tnd", onehot.astype(jnp.float32), values, precision=lax.Precision.HIGHEST
        )
    picker = (blocks[:, None] == jnp.arange(block_count, dtype=jnp.int32)[None, :]).astype(
        jnp.float32
    )
    summed = jnp.einsum("tb,tnd->bnd", picker, per_tile, precision=lax.Precision.HIGHEST)
    return summed.reshape(-1, values.shape[-1])


def shards(
    nodes_in,
    edge_latents,
    src_block,
    src_offset,
    dst_block,
    dst_offset,
    tile_counts,
    w_edge1,
    b_edge1,
    w_edge2,
    b_edge2,
    w_node1,
    b_node1,
    w_node2,
    b_node2,
    cotangent,
):
    peers = lax.axis_size("nodes")
    myself = lax.axis_index("nodes")
    nodes = nodes_in[0]
    cot = cotangent[0]
    node_rows, width = nodes.shape
    tile = src_offset.shape[-1]
    slots = src_offset.shape[3]
    block_count = node_rows // tile
    tiles_all = peers * slots
    scale_factor = float(lax.axis_size("events") * peers * node_rows) ** (-0.5)
    w_src, w_dst, w_lat = (w_edge1[:width], w_edge1[width : 2 * width], w_edge1[2 * width :])
    w_own, w_agg = (w_node1[:width], w_node1[width:])
    send_blocks = src_block[0, 0].reshape(-1)
    send_hot = tile_onehot(src_offset[0, 0].reshape(tiles_all, tile), tile)
    recv_blocks = dst_block[0, 0].reshape(-1)
    recv_hot = tile_onehot(dst_offset[0, 0].reshape(tiles_all, tile), tile)
    outgoing = gather_tiles(nodes, send_blocks, send_hot).reshape(peers, slots, tile, width)
    h_src = lax.all_to_all(outgoing, "nodes", split_axis=0, concat_axis=0, tiled=True).reshape(
        -1, width
    )
    counts = lax.dynamic_index_in_dim(tile_counts[0], myself, 1, keepdims=False)
    live = jnp.arange(slots, dtype=jnp.int32)[None, :] < counts[:, None]
    live = (
        jnp.broadcast_to(live[..., None], (peers, slots, tile)).reshape(-1, 1).astype(jnp.bfloat16)
    )
    lat = edge_latents[0, 0].reshape(-1, width)
    h_dst = gather_tiles(nodes, recv_blocks, recv_hot).reshape(-1, width)
    z_one = (
        jnp.dot(h_src, w_src, preferred_element_type=jnp.float32)
        + jnp.dot(h_dst, w_dst, preferred_element_type=jnp.float32)
        + jnp.dot(lat, w_lat, preferred_element_type=jnp.float32)
        + b_edge1
    )
    a_one = jax.nn.silu(z_one).astype(jnp.bfloat16)
    message = (jnp.dot(a_one, w_edge2, preferred_element_type=jnp.float32) + b_edge2).astype(
        jnp.bfloat16
    ) * live
    agg = scatter_tiles(
        message.reshape(tiles_all, tile, width), recv_blocks, recv_hot, block_count
    ).astype(jnp.bfloat16)
    z_two = (
        jnp.dot(nodes, w_own, preferred_element_type=jnp.float32)
        + jnp.dot(agg, w_agg, preferred_element_type=jnp.float32)
        + b_node1
    )
    a_two = jax.nn.silu(z_two).astype(jnp.bfloat16)
    updated = (
        nodes.astype(jnp.float32)
        + jnp.dot(a_two, w_node2, preferred_element_type=jnp.float32)
        + b_node2
    ).astype(jnp.bfloat16)
    g_two = (
        jnp.dot(cot, w_node2.T, preferred_element_type=jnp.float32) * silu_slope(z_two)
    ).astype(jnp.bfloat16)
    node_terms = (
        jnp.concatenate(
            [
                jnp.dot(nodes.T, g_two, preferred_element_type=jnp.float32),
                jnp.dot(agg.T, g_two, preferred_element_type=jnp.float32),
            ],
            axis=0,
        ),
        jnp.sum(g_two.astype(jnp.float32), axis=0),
        jnp.dot(a_two.T, cot, preferred_element_type=jnp.float32),
        jnp.sum(cot.astype(jnp.float32), axis=0),
    )
    g_agg = jnp.dot(g_two, w_agg.T, preferred_element_type=jnp.float32).astype(jnp.bfloat16)
    g_msg = gather_tiles(g_agg, recv_blocks, recv_hot).reshape(-1, width) * live
    g_one = (
        jnp.dot(g_msg, w_edge2.T, preferred_element_type=jnp.float32) * silu_slope(z_one)
    ).astype(jnp.bfloat16)
    g_src = jnp.dot(g_one, w_src.T, preferred_element_type=jnp.float32).reshape(
        peers, slots, tile, width
    )
    returned = (
        lax.all_to_all(g_src.astype(jnp.bfloat16), "nodes", split_axis=0, concat_axis=0, tiled=True)
        .astype(g_src.dtype)
        .reshape(-1, width)
    )
    g_dst = jnp.dot(g_one, w_dst.T, preferred_element_type=jnp.float32)
    total = cot.astype(jnp.float32) + jnp.dot(g_two, w_own.T, preferred_element_type=jnp.float32)
    total = total + scatter_tiles(
        g_dst.reshape(tiles_all, tile, width), recv_blocks, recv_hot, block_count
    )
    total = total + scatter_tiles(
        returned.reshape(tiles_all, tile, width), send_blocks, send_hot, block_count
    )
    edge_terms = (
        jnp.concatenate(
            [
                jnp.dot(h_src.T, g_one, preferred_element_type=jnp.float32),
                jnp.dot(h_dst.T, g_one, preferred_element_type=jnp.float32),
                jnp.dot(lat.T, g_one, preferred_element_type=jnp.float32),
            ],
            axis=0,
        ),
        jnp.sum(g_one.astype(jnp.float32), axis=0),
        jnp.dot(a_one.T, g_msg, preferred_element_type=jnp.float32),
        jnp.sum(g_msg.astype(jnp.float32), axis=0),
    )
    summed = lax.psum(
        (
            edge_terms[0],
            edge_terms[1],
            edge_terms[2],
            edge_terms[3],
            node_terms[0],
            node_terms[1],
            node_terms[2],
            node_terms[3],
        ),
        ("events", "nodes"),
    )
    scaled = [value * scale_factor for value in summed]
    return (
        updated[None],
        total.astype(jnp.bfloat16)[None],
        scaled[0],
        scaled[1],
        scaled[2],
        scaled[3],
        scaled[4],
        scaled[5],
        scaled[6],
        scaled[7],
    )


def solution(mesh):
    return jax.shard_map(
        shards,
        mesh=mesh,
        in_specs=(
            P("events", "nodes", None),
            P("events", "nodes", None, None, None, None),
            P("events", "nodes", None, None),
            P("events", "nodes", None, None, None),
            P("events", "nodes", None, None),
            P("events", "nodes", None, None, None),
            P("events", None, None),
            P(),
            P(),
            P(),
            P(),
            P(),
            P(),
            P(),
            P(),
            P("events", "nodes", None),
        ),
        out_specs=(
            P("events", "nodes", None),
            P("events", "nodes", None),
            P(),
            P(),
            P(),
            P(),
            P(),
            P(),
            P(),
            P(),
        ),
        check_vma=False,
    )
```

profile of v0, /device:TPU:1, one launch (start us, length us, event | category | flops | bytes accessed | tf_op | source)
XLA Modules:
  0.0 243.8 jit_solution(3081769146235548526)
XLA Ops:
  7.2 0.8 copy.33
  8.1 1.7 gather_fusion
  9.8 1.3 convolution_convert_fusion.4
  11.1 5.4 %all-to-all-start = ((bf16[8,2,128,128]{3,2,1,0:T(8,128)(2,1)}), bf16[8,2,128,128]{3,2,1,0:T(8,128)(2,1)S(1)}, u32[]{:S(2)}, u32[]{:S(2)}) async-start(bf16[8,2,128,128]{3,2,1,0:T(8,128)(2,1)} %bitcast.6), calls=%async_computation | async-start | bytes 1048576 | tf_op jit(solution)/shard_map/all_to_all | solution.py:75
  16.4 0.7 copy-done.22
  17.2 0.1 reshape_squeeze.15
  17.3 0.6 gather_fusion.1
  18.0 0.2 dynamic-slice_reduce_fusion
  18.2 0.5 copy-done.11
  18.7 0.5 convolution_convert_fusion.3
  19.2 0.7 eq.79
  20.0 0.1 reshape.170
  20.1 0.9 convert_reduce_fusion
  20.9 1.2 fusion.25
  22.2 1.0 all-to-all-done
  23.2 0.3 fusion.40
  23.4 0.3 convolution_add_fusion.5
  23.8 0.6 copy-done.28
  24.4 1.4 multiply_convert_fusion.1
  25.9 0.7 copy-done.29
  26.6 0.4 fusion.12
  27.0 1.0 fusion.20
  28.0 1.2 convolution_convert_fusion.5
  29.2 0.1 copy.35
  29.4 0.6 copy-done.30
  30.0 1.3 multiply_convert_fusion
  31.3 1.0 convert_reduce_fusion.1
  32.3 0.3 fusion.58
  32.6 0.3 convolution_bitcast_fusion
  33.0 1.1 convolution_convert_fusion.1
  34.1 2.5 %gather_fusion.2 = bf16[16,128,128]{2,1,0:T(8,128)(2,1)} fusion(bf16[16,128,128]{2,1,0:T(8,128)(2,1)} %bitcast.107, s32[1024]{0:T(1024)S(1)} %pad_clamp_fusion), kind=kCustom, calls=%fused_computation.2 | custom fusion | bytes 1048640 | tf_op jit(solution)/shard_map/gather | solution.py:20
  36.5 2.3 convert_reduce_fusion.2
  38.8 0.3 bitcast_multiply_fusion
  39.1 0.7 copy-done.6
  39.8 1.0 fusion.57
  40.8 1.0 convert_reduce_fusion.3
  41.8 0.3 fusion.56
  42.1 0.3 fusion.55
  42.5 0.3 convolution_bitcast_fusion.1
  42.9 0.5 copy-done.9
  43.4 1.1 convolution_convert_fusion
  44.5 0.3 fusion.36
  44.8 0.7 copy-done.3
  45.5 1.0 fusion.21
  46.5 1.1 fusion.11
  47.6 7.0 %all-to-all-start.1 = ((bf16[8,2,128,128]{3,2,1,0:T(8,128)(2,1)}), bf16[8,2,128,128]{3,2,1,0:T(8,128)(2,1)}, u32[]{:S(2)}, u32[]{:S(2)}) async-start(bf16[8,2,128,128]{3,2,1,0:T(8,128)(2,1)} %bitcast.104), calls=%async_computation.1 | async-start | bytes 1048576 | tf_op jit(solution)/shard_map/all_to_all | solution.py:133
  54.6 1.5 fusion.19
  56.2 2.2 fusion.15
  58.4 0.7 pad_maximum_fusion.1
  59.0 0.7 pad_maximum_fusion
  59.8 0.7 copy-done.21
  60.4 39.4 %all-reduce = (f32[128]{0:T(128)S(1)}, f32[128]{0:T(128)S(1)}, f32[128]{0:T(128)S(1)}, f32[128]{0:T(128)S(1)}) all-reduce(f32[128]{0:T(128)S(1)} %copy-done.26, f32[128]{0:T(128)S(1)} %copy-done.25, f32[128]{0:T(128)S(1)} %copy-done.24, f32[128]{0:T(128)S(1)} %copy-done.21), channel_id=1, replica_groups=mesh['events'=4,'nodes'=8] {'events','nodes'}, use_global_device_ids=true, to_apply=%region_2.3 | all-reduce | flops 512 | bytes 4096 | tf_op jit(solution)/shard_map/psum | solution.py:158
  99.9 0.5 broadcast_multiply_fusion.6
  100.4 1.6 copy.36
  102.0 0.5 broadcast_multiply_fusion.4
  102.5 126.7 %all-reduce.4.cloned.1.call-done = (f32[384,128]{1,0:T(8,128)}, f32[128,128]{1,0:T(8,128)}, f32[256,128]{1,0:T(8,128)}, f32[128,128]{1,0:T(8,128)}) async-done(((f32[384,128]{1,0:T(8,128)}, f32[128,128]{1,0:T(8,128)}, f32[256,128]{1,0:T(8,128)}, f32[128,128]{1,0:T(8,128)}), (f32[384,128]{1,0:T(8,128)}, f32[128,128]{1,0:T(8,128)}, f32[256,128]{1,0:T(8,128)}, ...) | async-done | bytes 458768 | tf_op jit(solution)/shard_map/psum | solution.py:158
  229.2 1.6 broadcast_multiply_fusion.1
  230.8 0.7 broadcast_multiply_fusion.2
  231.4 0.3 copy-done.7
  231.8 0.7 broadcast_multiply_fusion
  232.5 1.8 fusion.18
  234.2 1.2 fusion.13
  235.5 0.3 copy.38
  235.8 1.1 fusion.10
  (66 shorter events, 0.6 us)
Async XLA Ops:
  7.2 16.6 %copy-start = (bf16[1,1,8,2,128,128]{5,4,3,2,1,0:T(8,128)(2,1)S(1)}, bf16[1,1,8,2,128,128]{5,4,3,2,1,0:T(8,128)(2,1)}, u32[]{:S(2)}) copy-start(bf16[1,1,8,2,128,128]{5,4,3,2,1,0:T(8,128)(2,1)} %param.17) | copy-start | bytes 1572868
  8.1 1.7 copy-start.14
  11.1 6.2 %copy-start.1 = (bf16[1,2048,128]{2,1,0:T(8,128)(2,1)S(1)}, bf16[1,2048,128]{2,1,0:T(8,128)(2,1)}, u32[]{:S(2)}) copy-start(bf16[1,2048,128]{2,1,0:T(8,128)(2,1)} %param.16) | copy-start | bytes 1572868
  11.1 12.1 %all-to-all-start = ((bf16[8,2,128,128]{3,2,1,0:T(8,128)(2,1)}), bf16[8,2,128,128]{3,2,1,0:T(8,128)(2,1)S(1)}, u32[]{:S(2)}, u32[]{:S(2)}) async-start(bf16[8,2,128,128]{3,2,1,0:T(8,128)(2,1)} %bitcast.6), calls=%async_computation | async-start | bytes 1048576 | tf_op jit(solution)/shard_map/all_to_all | solution.py:75
  16.4 0.7 copy-start.22
  17.3 0.7 copy-start.19
  18.0 0.7 copy-start.11
  18.7 1.4 copy-start.2
  20.0 8.0 %copy-start.17 = (s32[16]{0:T(128)}, s32[16]{0:T(128)S(1)}, u32[]{:S(2)}) copy-start(s32[16]{0:T(128)S(1)} %eq.32) | copy-start | bytes 196
  20.0 0.9 copy-start.10
  20.9 2.2 copy-start.8
  23.7 0.7 copy-start.28
  24.4 1.5 copy-start.27
  25.8 1.1 copy-start.5
  25.9 0.7 copy-start.29
  28.0 1.4 copy-start.4
  29.3 0.7 copy-start.30
  30.0 1.3 copy-start.15
  38.8 1.0 copy-start.6
  38.8 2.0 copy-start.31
  42.5 0.9 copy-start.9
  44.5 1.0 copy-start.3
  45.5 1.0 copy-start.16
  45.5 1.0 copy-start.23
  47.6 184.8 %all-to-all-start.1 = ((bf16[8,2,128,128]{3,2,1,0:T(8,128)(2,1)}), bf16[8,2,128,128]{3,2,1,0:T(8,128)(2,1)}, u32[]{:S(2)}, u32[]{:S(2)}) async-start(bf16[8,2,128,128]{3,2,1,0:T(8,128)(2,1)} %bitcast.104), calls=%async_computation.1 | async-start | bytes 1048576 | tf_op jit(solution)/shard_map/all_to_all | solution.py:133
  54.6 174.6 %all-reduce.4.cloned.1.call-start = ((), (), s32[]{:S(2)}) async-start(), calls=%async_computation.2 | async-start | bytes 917504 | tf_op jit(solution)/shard_map/psum | solution.py:158
  54.6 1.5 copy-start.18
  59.0 0.7 copy-start.26
  59.7 0.7 copy-start.21
  59.7 0.7 copy-start.24
  59.7 0.7 copy-start.25
  229.2 1.6 copy-start.12
  229.2 1.6 copy-start.13
  230.8 1.0 copy-start.7
  232.4 1.8 copy-start.20
Sparse Core Ops, SparseCore 0:
  100.0 129.1 all-reduce.3
where the time goes:
time: 245 us; the launch traced here: 244 us
  waiting for transfers between devices  128 us (52%)
  blocking collectives  39.4 us (16%)
  matrix products  28.1 us (11%)
  local copies, waits for them, and re-layouts  15.2 us (6%)
  between operations  14.3 us (6%)
  starting transfers between devices  12.4 us (5%)
  other arithmetic  6.65 us (3%)
    psum x1, waiting for transfers between devices, shards(): lax.psum((edge_terms[0], edge_terms[1], edge_terms[2], edge_terms[3], nod...  127 us
    psum x1, blocking collectives, shards(): lax.psum((edge_terms[0], edge_terms[1], edge_terms[2], edge_terms[3], nod...  39.4 us
    unnamed x66, local copies, waits for them, and re-layouts  7.1 us
    all_to_all x1, starting transfers between devices, shards(): lax.all_to_all(g_src.astype(jnp.bfloat16), 'nodes', split_axis=0, concat_...  7.01 us
    all_to_all x1, starting transfers between devices, shards(): lax.all_to_all(outgoing, 'nodes', split_axis=0, concat_axis=0, tiled=True)  5.35 us
  transfers between devices with their start and end apart: 3, of which 2 were waited for; matrix products, arithmetic and copies ran while one was open for 6% of the time, Pallas kernels for 0%

commit v1 on v0

--- a/solution.py
+++ b/solution.py
@@ -2,6 +2,18 @@
 import jax.numpy as jnp
 from jax import lax
 from jax.sharding import PartitionSpec as P
+
+
+def exchange_directly(x, axis, split, join):
+    ways, here = (lax.axis_size(axis), lax.axis_index(axis))
+    width = x.shape[split] // ways
+    turned = jnp.roll(x, -here * width, axis=split)
+    got = [lax.slice_in_dim(turned, 0, width, axis=split)]
+    for far in range(1, ways):
+        sent = lax.slice_in_dim(turned, far * width, (far + 1) * width, axis=split)
+        got.append(lax.ppermute(sent, axis, [(d, (d + far) % ways) for d in range(ways)]))
+    line = jnp.concatenate(got[::-1], axis=join)
+    return jnp.roll(line, (here + 1) * got[0].shape[join], axis=join)
 
 
 def silu_slope(value):
@@ -130,7 +142,7 @@
         peers, slots, tile, width
     )
     returned = (
-        lax.all_to_all(g_src.astype(jnp.bfloat16), "nodes", split_axis=0, concat_axis=0, tiled=True)
+        exchange_directly(g_src.astype(jnp.bfloat16), "nodes", 0, 0)
         .astype(g_src.dtype)
         .reshape(-1, width)
     )

time: 245 us -> 244 us (level)
  waiting for transfers between devices: 128 us -> 117 us
  local copies, waits for them, and re-layouts: 15.2 us -> 19.4 us
  other arithmetic: 6.65 us -> 9.63 us
  starting transfers between devices: 12.4 us -> 14.9 us
    psum x1, waiting for transfers between devices: 127 us -> 111 us  [shards(): lax.psum((edge_terms[0], edge_terms[1], edge_terms[2], edge_terms[3], nod...]
    ppermute x0 -> x7, starting transfers between devices: none -> 9.55 us  [exchange_directly(): lax.ppermute(sent, axis, [(d, (d + far) % ways) for d in range(ways)])]
    all_to_all x1 -> x0, starting transfers between devices: 7.01 us -> none  [shards(): lax.all_to_all(g_src.astype(jnp.bfloat16), 'nodes', split_axis=0, concat_...]
    unnamed x66 -> x75, local copies, waits for them, and re-layouts: 7.1 us -> 11.9 us
    ppermute x0 -> x7, waiting for transfers between devices: none -> 4.01 us  [exchange_directly(): lax.ppermute(sent, axis, [(d, (d + far) % ways) for d in range(ways)])]
    mul x5 -> x8, other arithmetic: 3.99 us -> 5.64 us  [shards(): scaled = [value * scale_factor for value in summed]]
  transfers between devices with their start and end apart: 3 -> 9, of which waited for: 2 -> 4; matrix products, arithmetic and copies ran while one was open for 6% -> 7% of each run, Pallas kernels for 0% -> 0%
where the time goes in v1:
time: 244 us; the launch traced here: 243 us
  waiting for transfers between devices  117 us (48%)
  blocking collectives  41.2 us (17%)
  matrix products  26.2 us (11%)
  local copies, waits for them, and re-layouts  19.4 us (8%)
  starting transfers between devices  14.9 us (6%)
  between operations  14.4 us (6%)
  other arithmetic  9.63 us (4%)
    psum x1, waiting for transfers between devices, shards(): lax.psum((edge_terms[0], edge_terms[1], edge_terms[2], edge_terms[3], nod...  111 us
    psum x1, blocking collectives, shards(): lax.psum((edge_terms[0], edge_terms[1], edge_terms[2], edge_terms[3], nod...  41.2 us
    unnamed x75, local copies, waits for them, and re-layouts  11.9 us
    ppermute x7, starting transfers between devices, exchange_directly(): lax.ppermute(sent, axis, [(d, (d + far) % ways) for d in range(ways)])  9.55 us
    mul x8, other arithmetic, shards(): scaled = [value * scale_factor for value in summed]  5.64 us
    all_to_all x1, starting transfers between devices, shards(): lax.all_to_all(outgoing, 'nodes', split_axis=0, concat_axis=0, tiled=True)  5.35 us
  transfers between devices with their start and end apart: 9, of which 4 were waited for; matrix products, arithmetic and copies ran while one was open for 7% of the time, Pallas kernels for 0%

profile of v1, /device:TPU:1, one launch (start us, length us, event | category | flops | bytes accessed | tf_op | source)
XLA Modules:
  0.0 243.0 jit_solution(7660917823203948791)
XLA Ops:
  7.2 0.8 copy.33
  8.1 0.6 copy-done.24
  8.9 1.7 gather_fusion
  10.6 1.3 convolution_convert_fusion.4
  11.8 5.4 %all-to-all-start = ((bf16[8,2,128,128]{3,2,1,0:T(8,128)(2,1)}), bf16[8,2,128,128]{3,2,1,0:T(8,128)(2,1)S(1)}, u32[]{:S(2)}, u32[]{:S(2)}) async-start(bf16[8,2,128,128]{3,2,1,0:T(8,128)(2,1)} %bitcast.6), calls=%async_computation | async-start | bytes 1048576 | tf_op jit(solution)/shard_map/all_to_all | solution.py:87
  17.2 0.6 gather_fusion.1
  18.1 0.5 copy-done.11
  19.1 0.6 eq.81
  19.9 0.8 convert_reduce_fusion
  20.7 1.2 fusion.27
  22.0 2.0 all-to-all-done
  24.5 0.6 copy-done.29
  25.2 1.4 multiply_convert_fusion.1
  26.7 0.7 copy-done.30
  27.7 1.0 fusion.20
  28.7 1.2 convolution_convert_fusion.5
  30.1 0.6 copy-done.31
  30.7 1.2 multiply_convert_fusion
  32.0 1.0 convert_reduce_fusion.1
  33.7 1.1 convolution_convert_fusion.1
  34.8 2.5 %gather_fusion.2 = bf16[16,128,128]{2,1,0:T(8,128)(2,1)} fusion(bf16[16,128,128]{2,1,0:T(8,128)(2,1)} %bitcast.108, s32[1024]{0:T(1024)S(1)} %pad_clamp_fusion), kind=kCustom, calls=%fused_computation.2 | custom fusion | bytes 1048640 | tf_op jit(solution)/shard_map/gather | solution.py:32
  37.2 2.3 convert_reduce_fusion.2
  39.8 0.7 copy-done.6
  40.5 1.0 fusion.60
  41.5 1.0 convert_reduce_fusion.3
  43.6 0.5 copy-done.8
  44.1 1.1 convolution_convert_fusion
  45.5 0.7 copy-done.3
  46.3 1.0 fusion.23
  47.2 1.1 fusion.11
  48.3 0.6 copy-done.23
  49.0 41.2 %all-reduce = (f32[128]{0:T(128)S(1)}, f32[128]{0:T(128)S(1)}, f32[128]{0:T(128)S(1)}, f32[128]{0:T(128)S(1)}) all-reduce(f32[128]{0:T(128)} %get-tuple-element.30, f32[128]{0:T(128)S(1)} %copy-done.27, f32[128]{0:T(128)S(1)} %copy-done.26, f32[128]{0:T(128)S(1)} %copy-done.23), channel_id=1, replica_groups=mesh['events'=4,'nodes'=8] {'events','nodes'}, use_global_device_ids=true, to_apply=%region_2.4 | all-reduce | flops 512 | bytes 4096 | tf_op jit(solution)/shard_map/psum | solution.py:170
  90.2 0.5 broadcast_multiply_fusion.7
  90.7 0.5 broadcast_multiply_fusion.6
  91.2 0.5 broadcast_multiply_fusion.5
  91.7 0.5 broadcast_multiply_fusion.4
  92.3 1.2 fusion.22
  93.5 0.8 fusion.57
  94.2 3.4 %collective-permute-start.6 = (bf16[1,2,128,128]{3,2,1,0:T(8,128)(2,1)}, bf16[1,2,128,128]{3,2,1,0:T(8,128)(2,1)}, u32[]{:S(2)}, u32[]{:S(2)}) collective-permute-start(bf16[1,2,128,128]{3,2,1,0:T(8,128)(2,1)} %get-tuple-element.19), channel_id=1, source_target_pairs={{0,1},{1,2},{2,3},{3,4},{4,5},{5,6},{6,7},{7,0},{8,9},{9,10},{10,1... | collective-permute-start | bytes 196616 | tf_op jit(solution)/shard_map/ppermute | solution.py:14
  97.6 1.2 collective-permute-start.5
  98.8 0.6 collective-permute-start.3
  99.4 1.5 collective-permute-start
  100.9 1.5 fusion.19
  102.5 1.2 fusion.15
  104.0 0.7 pad_maximum_fusion
  104.7 0.7 pad_maximum_fusion.1
  105.4 0.8 copy-done.13
  106.2 0.6 collective-permute-start.1
  106.9 0.8 constant_dynamic-update-slice_fusion.6
  107.7 2.3 collective-permute-done.1
  110.0 2.2 collective-permute-start.2
  112.2 1.7 collective-permute-done.2
  114.0 0.9 constant_dynamic-update-slice_fusion.3
  114.8 0.9 constant_dynamic-update-slice_fusion.2
  115.7 0.9 constant_dynamic-update-slice_fusion.1
  116.6 0.9 constant_dynamic-update-slice_fusion
  117.7 1.0 fusion.18
  118.7 1.2 fusion.13
  120.2 1.1 fusion.10
  121.3 111.2 %all-reduce.4.cloned.1.call-done = (f32[384,128]{1,0:T(8,128)}, f32[128,128]{1,0:T(8,128)}, f32[256,128]{1,0:T(8,128)}, f32[128,128]{1,0:T(8,128)}) async-done(((f32[384,128]{1,0:T(8,128)}, f32[128,128]{1,0:T(8,128)}, f32[256,128]{1,0:T(8,128)}, f32[128,128]{1,0:T(8,128)}), (f32[384,128]{1,0:T(8,128)}, f32[128,128]{1,0:T(8,128)}, f32[256,128]{1,0:T(8,128)}, ...) | async-done | bytes 458768 | tf_op jit(solution)/shard_map/psum | solution.py:170
  232.6 1.7 broadcast_multiply_fusion
  234.2 0.6 broadcast_multiply_fusion.3
  234.9 0.6 broadcast_multiply_fusion.2
  235.5 0.7 broadcast_multiply_fusion.1
  (93 shorter events, 5.7 us)
Async XLA Ops:
  7.2 17.3 %copy-start = (bf16[1,1,8,2,128,128]{5,4,3,2,1,0:T(8,128)(2,1)S(1)}, bf16[1,1,8,2,128,128]{5,4,3,2,1,0:T(8,128)(2,1)}, u32[]{:S(2)}) copy-start(bf16[1,1,8,2,128,128]{5,4,3,2,1,0:T(8,128)(2,1)} %param.19) | copy-start | bytes 1572868
  8.0 0.7 copy-start.24
  8.9 1.7 copy-start.16
  11.8 5.4 %copy-start.1 = (bf16[1,2048,128]{2,1,0:T(8,128)(2,1)S(1)}, bf16[1,2048,128]{2,1,0:T(8,128)(2,1)}, u32[]{:S(2)}) copy-start(bf16[1,2048,128]{2,1,0:T(8,128)(2,1)} %param.18) | copy-start | bytes 1572868
  11.8 12.1 %all-to-all-start = ((bf16[8,2,128,128]{3,2,1,0:T(8,128)(2,1)}), bf16[8,2,128,128]{3,2,1,0:T(8,128)(2,1)S(1)}, u32[]{:S(2)}, u32[]{:S(2)}) async-start(bf16[8,2,128,128]{3,2,1,0:T(8,128)(2,1)} %bitcast.6), calls=%async_computation | async-start | bytes 1048576 | tf_op jit(solution)/shard_map/all_to_all | solution.py:87
  17.2 215.4 %all-reduce.4.cloned.1.call-start = ((), (), s32[]{:S(2)}) async-start(), calls=%async_computation.1 | async-start | bytes 917504 | tf_op jit(solution)/shard_map/psum | solution.py:170
  17.2 0.7 copy-start.21
  17.9 0.7 copy-start.11
  18.6 1.3 copy-start.2
  19.8 8.9 %copy-start.19 = (s32[16]{0:T(128)}, s32[16]{0:T(128)S(1)}, u32[]{:S(2)}) copy-start(s32[16]{0:T(128)S(1)} %eq.34) | copy-start | bytes 196
  19.9 0.8 copy-start.9
  20.7 3.2 %copy-start.7 = (bf16[384,128]{1,0:T(8,128)(2,1)S(1)}, bf16[384,128]{1,0:T(8,128)(2,1)}, u32[]{:S(2)}) copy-start(bf16[384,128]{1,0:T(8,128)(2,1)} %param.25) | copy-start | bytes 294916
  24.5 0.7 copy-start.29
  25.2 1.5 copy-start.28
  26.6 1.1 copy-start.5
  26.6 0.7 copy-start.30
  28.7 1.4 copy-start.4
  30.1 0.7 copy-start.31
  30.7 1.3 copy-start.17
  39.5 1.0 copy-start.6
  39.5 2.0 copy-start.32
  43.2 0.9 copy-start.8
  45.2 1.0 copy-start.3
  46.3 1.0 copy-start.18
  46.3 1.0 copy-start.25
  48.3 0.7 copy-start.23
  48.3 0.7 copy-start.26
  48.3 0.7 copy-start.27
  94.2 22.3 %collective-permute-start.6 = (bf16[1,2,128,128]{3,2,1,0:T(8,128)(2,1)}, bf16[1,2,128,128]{3,2,1,0:T(8,128)(2,1)}, u32[]{:S(2)}, u32[]{:S(2)}) collective-permute-start(bf16[1,2,128,128]{3,2,1,0:T(8,128)(2,1)} %get-tuple-element.19), channel_id=1, source_target_pairs={{0,1},{1,2},{2,3},{3,4},{4,5},{5,6},{6,7},{7,0},{8,9},{9,10},{10,1... | collective-permute-start | bytes 196616 | tf_op jit(solution)/shard_map/ppermute | solution.py:14
  97.6 18.1 %collective-permute-start.5 = (bf16[1,2,128,128]{3,2,1,0:T(8,128)(2,1)}, bf16[1,2,128,128]{3,2,1,0:T(8,128)(2,1)}, u32[]{:S(2)}, u32[]{:S(2)}) collective-permute-start(bf16[1,2,128,128]{3,2,1,0:T(8,128)(2,1)} %get-tuple-element.20), channel_id=1, source_target_pairs={{0,2},{1,3},{2,4},{3,5},{4,6},{5,7},{6,0},{7,1},{8,10},{9,11},{10,... | collective-permute-start | bytes 196616 | tf_op jit(solution)/shard_map/ppermute | solution.py:14
  98.8 16.0 %collective-permute-start.4 = (bf16[1,2,128,128]{3,2,1,0:T(8,128)(2,1)}, bf16[1,2,128,128]{3,2,1,0:T(8,128)(2,1)}, u32[]{:S(2)}, u32[]{:S(2)}) collective-permute-start(bf16[1,2,128,128]{3,2,1,0:T(8,128)(2,1)} %get-tuple-element.21), channel_id=1, source_target_pairs={{0,3},{1,4},{2,5},{3,6},{4,7},{5,0},{6,1},{7,2},{8,11},{9,12},{10,... | collective-permute-start | bytes 196616 | tf_op jit(solution)/shard_map/ppermute | solution.py:14
  98.8 15.2 %collective-permute-start.3 = (bf16[1,2,128,128]{3,2,1,0:T(8,128)(2,1)}, bf16[1,2,128,128]{3,2,1,0:T(8,128)(2,1)}, u32[]{:S(2)}, u32[]{:S(2)}) collective-permute-start(bf16[1,2,128,128]{3,2,1,0:T(8,128)(2,1)} %get-tuple-element.22), channel_id=1, source_target_pairs={{0,4},{1,5},{2,6},{3,7},{4,0},{5,1},{6,2},{7,3},{8,12},{9,13},{10,... | collective-permute-start | bytes 196616 | tf_op jit(solution)/shard_map/ppermute | solution.py:14
  99.4 6.0 %collective-permute-start = (bf16[1,2,128,128]{3,2,1,0:T(8,128)(2,1)}, bf16[1,2,128,128]{3,2,1,0:T(8,128)(2,1)}, u32[]{:S(2)}, u32[]{:S(2)}) collective-permute-start(bf16[1,2,128,128]{3,2,1,0:T(8,128)(2,1)} %get-tuple-element.25), channel_id=1, source_target_pairs={{0,7},{1,0},{2,1},{3,2},{4,3},{5,4},{6,5},{7,6},{8,15},{9,8},{10,9... | collective-permute-start | bytes 196616 | tf_op jit(solution)/shard_map/ppermute | solution.py:14
  100.9 1.5 copy-start.20
  105.4 0.8 copy-start.13
  106.2 3.7 %copy-start.12 = (bf16[1,2,128,128]{3,2,1,0:T(8,128)(2,1)S(1)}, bf16[1,2,128,128]{3,2,1,0:T(8,128)(2,1)}, u32[]{:S(2)}) copy-start(bf16[1,2,128,128]{3,2,1,0:T(8,128)(2,1)} %get-tuple-element.23) | copy-start | bytes 196612
  106.2 3.7 %collective-permute-start.1 = (bf16[1,2,128,128]{3,2,1,0:T(8,128)(2,1)S(1)}, bf16[1,2,128,128]{3,2,1,0:T(8,128)(2,1)S(1)}, u32[]{:S(2)}, u32[]{:S(2)}) collective-permute-start(bf16[1,2,128,128]{3,2,1,0:T(8,128)(2,1)S(1)} %copy-done.13), channel_id=1, source_target_pairs={{0,6},{1,7},{2,0},{3,1},{4,2},{5,3},{6,4},{7,5},{8,14},{9,15},{10,... | collective-permute-start | bytes 196616 | tf_op jit(solution)/shard_map/ppermute | solution.py:14
  110.0 4.0 %collective-permute-start.2 = (bf16[1,2,128,128]{3,2,1,0:T(8,128)(2,1)S(1)}, bf16[1,2,128,128]{3,2,1,0:T(8,128)(2,1)S(1)}, u32[]{:S(2)}, u32[]{:S(2)}) collective-permute-start(bf16[1,2,128,128]{3,2,1,0:T(8,128)(2,1)S(1)} %copy-done.12), channel_id=1, source_target_pairs={{0,5},{1,6},{2,7},{3,0},{4,1},{5,2},{6,3},{7,4},{8,13},{9,14},{10,... | collective-permute-start | bytes 196616 | tf_op jit(solution)/shard_map/ppermute | solution.py:14
  117.7 1.0 copy-start.22
  232.6 1.7 copy-start.15
  232.6 2.3 copy-start.14
  234.2 1.3 copy-start.10
Sparse Core Ops, SparseCore 0:
  105.5 126.9 all-reduce.3
